TPU v7x, 32 devices: a whole 2x2x4 slice. The times are simulated.
32 devices in a mesh: groups: 2 (over x), tiles: 16 (over z, y, core).
Axes of the slice: x: 2, y: 2, z: 4, core: 2. Of those that a mesh axis runs over, the one named last changes fastest.
Arguments:
- control: float32 [6, 64, 256, 128], P('groups', None, 'tiles'), parts along dimension 0, may hold values from -6 to 6
- departures: float32 [2048, 768], P(('groups', 'tiles')), parts along dimension 0, may hold values from -6 to 6
- obs_cell: int32 [2048], P(('groups', 'tiles')), parts along dimension 0, may hold values from 0 to 2047
- obs_owner: int32 [2048, 1], P(('groups', 'tiles')), parts along dimension 0, may hold values from 0 to 15; in each aligned block of 64 rows (0 to 63, 64 to 127, ...) at most 8 rows name the same one
- scale_class: int32 [256, 128], P('tiles'), may hold values from 0 to 7
- sea_mask: int32 [256, 128], P('tiles'), may hold values 0 or 1
- class_table: float32 [2, 8], replicated, may hold values from 0.02 to 0.24
- obs_precision: float32 [3072, 192], P('tiles'), as said below
Outputs:
- increment: float32 [6, 64, 256, 128], P('groups', None, 'tiles'), parts along dimension 0
- gradient: float32 [6, 64, 256, 128], P('groups', None, 'tiles'), parts along dimension 0
There are 2 independent parts, one for each index of `groups`. A program takes and returns all parts, laid end to end along the dimension named above; an argument that names none is the same for every part. Nothing has to cross between parts.
Inputs may be any that keep to these rules, and one draw needn't show every extreme that they name: `obs_owner`: among the profiles of one tile no owner is named more than 8 times; some owner exactly 8 times. `obs_precision`: each owner's block is symmetric and positive definite.
All inputs are finite; a program needn't handle non-finite values. No bound on the sum of `sea_mask` on one device may be relied on, other than what follows from the above.
Results may differ from a plain program's by a relative error of at most 0.00015.
Values sent between devices are 32-bit elements; how exact they have to be, the bound alone decides.
A program may use at most 64 MiB of HBM per device.

v0:
```python
import functools
import jax
import jax.numpy as jnp
from jax import lax
from jax.experimental import pallas as pl
from jax.experimental.pallas import tpu as pltpu
from jax.sharding import PartitionSpec as P

STEPS = 8
MEMBERS = 4
CHUNKS = 6
HIGHEST = lax.Precision.HIGHEST
F32 = jnp.float32
BF16 = jnp.bfloat16
I32 = jnp.int32


def sweep(load_row, fx_ref, fy_ref, emit, rows):
    current = [None] * (STEPS + 1)
    flux = [None] * (STEPS + 1)
    for i in range(rows):
        value = load_row(i)
        for s in range(1, STEPS + 1):
            before, current[s] = current[s], value
            if before is None:
                break
            r = i - s
            flux_x = fx_ref[r] * (value - before)
            last, flux[s] = flux[s], flux_x
            if last is None:
                break
            flux_y = fy_ref[r] * (pltpu.roll(before, before.shape[1] - 1, 1) - before)
            value = before + ((flux_x - last) + (flux_y - pltpu.roll(flux_y, 1, 1)))
        else:
            emit(i - STEPS, value)


def split(x):
    high = x.astype(BF16)
    return high, (x - high.astype(F32)).astype(BF16)


def observe_kernel(
    tiles, cap, chan, cx,
    table, control, departures, cell_ref, owner_ref, class_ref, mask_ref, precision_ref,
    inc_out, back_out, cells_out, fxb, fyb, ocb,
    own, halo_l, halo_r, inc, geo, geo_l, geo_r, cells, cells_in, hot, model_t,
    dep_send, dep_recv, mod_send, mod_recv, ans, back, weighted_dep,
    local_sem, out_sem, back_sem, halo_send, halo_recv, geo_send, geo_recv, a2a_send, a2a_recv,
):
    me = lax.axis_index("tiles")
    h = STEPS
    ext = cx + 2 * h
    slots = tiles * cap
    nc = chan // CHUNKS
    ny = own.shape[2]
    right = lax.rem(me + 1, tiles)
    left = lax.rem(me + tiles - 1, tiles)

    own_copy = pltpu.make_async_copy(control, own, local_sem)
    own_copy.start()
    geo[0] = class_ref[...]
    geo[1] = mask_ref[...]

    barrier = pltpu.get_barrier_semaphore()

    @pl.loop(1, tiles)
    def _(k):
        pl.semaphore_signal(barrier, inc=1, device_id={"tiles": lax.rem(me + k, tiles)}, device_id_type=pl.DeviceIdType.MESH)

    pl.semaphore_wait(barrier, tiles - 1)

    def remote(src, dst, send, recv, to):
        return pltpu.make_async_remote_copy(
            src_ref=src, dst_ref=dst, send_sem=send, recv_sem=recv,
            device_id={"tiles": to}, device_id_type=pl.DeviceIdType.MESH,
        )

    geo_copies = [
        remote(geo.at[:, pl.ds(cx - h, h)], geo_l, geo_send.at[0], geo_recv.at[0], right),
        remote(geo.at[:, pl.ds(0, h)], geo_r, geo_send.at[1], geo_recv.at[1], left),
    ]
    for copy in geo_copies:
        copy.start()
    halo_copies = []
    for q in range(CHUNKS):
        part = pl.ds(q * nc, nc)
        pair = [
            remote(control.at[part, pl.ds(cx - h, h)], halo_l.at[part], halo_send.at[0, q], halo_recv.at[0, q], right),
            remote(control.at[part, pl.ds(0, h)], halo_r.at[part], halo_send.at[1, q], halo_recv.at[1, q], left),
        ]
        for copy in pair:
            copy.start()
        halo_copies.append(pair)

    n = departures.shape[0]
    eye = lax.broadcasted_iota(I32, (n, n), 0) == lax.broadcasted_iota(I32, (n, n), 1)
    lower = lax.broadcasted_iota(I32, (n, n), 1) < lax.broadcasted_iota(I32, (n, n), 0)
    owner_row = owner_ref[...]
    owner_col = jnp.sum(jnp.where(eye, owner_row, 0), axis=1, keepdims=True)
    cell_col = jnp.sum(jnp.where(eye, cell_ref[...], 0), axis=1, keepdims=True)
    slot_col = jnp.sum(jnp.where((owner_col == owner_row) & lower, 1, 0), axis=1, keepdims=True)
    offset = owner_col - me
    offset = jnp.where(offset < 0, offset + tiles, offset)
    dest_col = offset * cap + slot_col
    dest_row = jnp.sum(jnp.where(eye, dest_col, 0), axis=0, keepdims=True)
    place = jnp.where(lax.broadcasted_iota(I32, (slots, n), 0) == dest_row, 1.0, 0.0).astype(F32)
    spread = jnp.dot(place, departures[...], precision=HIGHEST, preferred_element_type=F32)
    dep_send[...] = spread.reshape(dep_send.shape)

    def exchange(src_of, dst, phase):
        @pl.loop(1, tiles)
        def _(k):
            src, to = src_of(k)
            remote(src, dst.at[k], a2a_send.at[phase], a2a_recv.at[phase], to).start()

    def landed(buffer, sem):
        pltpu.make_async_copy(buffer.at[pl.ds(1, tiles - 1)], buffer.at[pl.ds(1, tiles - 1)], sem).wait()

    exchange(lambda k: (dep_send.at[k], lax.rem(me + k, tiles)), dep_recv, 0)
    dep_recv[0] = dep_send[0]

    slot_lane = lax.broadcasted_iota(I32, (n, slots), 1)

    def cell_row(dest):
        return jnp.sum(jnp.where(dest == slot_lane, cell_col + 1, 0), axis=0, keepdims=True) - 1

    later = jnp.where(offset + 1 == tiles, 0, offset + 1) * cap + slot_col
    sooner = jnp.where(offset == 0, tiles - 1, offset - 1) * cap + slot_col
    mine = cell_row(dest_col)
    for j, row in enumerate((cell_row(later), mine, cell_row(sooner))):
        cells[j] = jnp.broadcast_to(row, cells.shape[1:])
    cell_copies = [
        remote(cells.at[0], cells_in.at[0], geo_send.at[2], geo_recv.at[2], left),
        remote(cells.at[2], cells_in.at[1], geo_send.at[3], geo_recv.at[3], right),
    ]
    for copy in cell_copies:
        copy.start()
    for j in range(cx // 2):
        index = lax.broadcasted_iota(I32, (2 * ny, slots), 0) + 2 * j * ny
        hot[j] = jnp.where(index == mine, 1.0, 0.0).astype(BF16)

    for copy in geo_copies:
        copy.wait()
    kinds = jnp.concatenate([geo_l[0], geo[0], geo_r[0]], axis=0)
    ocean = jnp.concatenate([geo_l[1], geo[1], geo_r[1]], axis=0).astype(F32)
    kx = jnp.zeros((ext, ny), F32)
    ky = jnp.zeros((ext, ny), F32)
    for c in range(table.shape[1]):
        kx = jnp.where(kinds == c, table[0, c], kx)
        ky = jnp.where(kinds == c, table[1, c], ky)
    face_x = 0.5 * (kx + pltpu.roll(kx, ext - 1, 0)) * ocean * pltpu.roll(ocean, ext - 1, 0)
    face_y = 0.5 * (ky + pltpu.roll(ky, ny - 1, 1)) * ocean * pltpu.roll(ocean, ny - 1, 1)
    face_y = jnp.where(lax.broadcasted_iota(I32, (ext, ny), 1) < ny - 1, face_y, 0.0)
    for r in range(ext):
        fxb[r] = jnp.broadcast_to(face_x[r : r + 1], (8, ny))
        fyb[r] = jnp.broadcast_to(face_y[r : r + 1], (8, ny))
        ocb[r] = jnp.broadcast_to(ocean[r : r + 1], (8, ny))

    own_copy.wait()
    own2, left2, right2, inc2 = (
        own.reshape(chan * cx, ny), halo_l.reshape(chan * h, ny), halo_r.reshape(chan * h, ny), inc.reshape(chan * cx, ny)
    )
    inc_copies = []
    for q in range(CHUNKS):
        for copy in halo_copies[q]:
            copy.wait_recv()

        @pl.loop(q * nc // 8, (q + 1) * nc // 8)
        def _(g):
            def load_row(i):
                if i < h:
                    row = left2[pl.ds(g * 8 * h + i, 8, stride=h), :]
                elif i < h + cx:
                    row = own2[pl.ds(g * 8 * cx + i - h, 8, stride=cx), :]
                else:
                    row = right2[pl.ds(g * 8 * h + i - h - cx, 8, stride=h), :]
                return ocb[i] * row

            def emit(r, value):
                inc2[pl.ds(g * 8 * cx + r - h, 8, stride=cx), :] = value

            sweep(load_row, fxb, fyb, emit, ext)

        part = pl.ds(q * nc, nc)
        copy = pltpu.make_async_copy(inc.at[part], inc_out.at[part], out_sem.at[q])
        copy.start()
        inc_copies.append(copy)
        total = jnp.zeros((nc, slots), F32)
        for j in range(cx // 2):
            pair = jnp.concatenate(
                [inc2[pl.ds(q * nc * cx + 2 * j + b, nc, stride=cx), :] for b in range(2)], axis=1
            )
            for piece in split(pair):
                total += jnp.dot(piece, hot[j], preferred_element_type=F32)
        model_t[part] = total

    mod_send[...] = model_t[...].T.reshape(mod_send.shape)
    exchange(lambda k: (mod_send.at[k], lax.rem(me + k, tiles)), mod_recv, 1)
    mod_recv[0] = mod_send[0]
    precision = precision_ref[...]
    landed(dep_recv, a2a_recv.at[0])
    for m in range(MEMBERS):
        rows = dep_recv[:, :, m * chan : (m + 1) * chan].reshape(slots, chan)
        weighted_dep[m] = jnp.dot(rows, precision, precision=HIGHEST, preferred_element_type=F32)
    landed(mod_recv, a2a_recv.at[1])
    model = mod_recv[...].reshape(slots, chan)
    weighted_model = jnp.dot(model, precision, precision=HIGHEST, preferred_element_type=F32)
    answer = jnp.zeros((slots, chan), F32)
    for m in range(MEMBERS):
        misfit = model - dep_recv[:, :, m * chan : (m + 1) * chan].reshape(slots, chan)
        weighted = weighted_model - weighted_dep[m]
        energy = jnp.sum(misfit * weighted, axis=1, keepdims=True) / chan
        answer += weighted / (1.0 + energy)
    answer = answer.reshape(tiles, cap, chan)
    ans[pl.ds(1, tiles)] = answer
    ans[0] = answer[tiles - 1]
    ans[tiles + 1] = answer[0]
    exchange(lambda k: (ans.at[pl.ds(k, 3)], lax.rem(me - k + tiles, tiles)), back, 2)
    for j in range(3):
        back[0, j] = ans[j]
    for copy in cell_copies:
        copy.wait()
    cells_out[0] = cells_in[0]
    cells_out[1] = cells[1]
    cells_out[2] = cells_in[1]
    for pair in halo_copies:
        for copy in pair:
            copy.wait_send()
    landed(dep_recv, a2a_send.at[0])
    landed(mod_recv, a2a_send.at[1])
    for copy in inc_copies:
        copy.wait()
    landed(back, a2a_recv.at[2])
    landed(back, a2a_send.at[2])
    copy = pltpu.make_async_copy(back, back_out, back_sem)
    copy.start()
    copy.wait()


def adjoint_kernel(
    chan, cx,
    control, inc_in, back, cells, fxb, fyb, ocb,
    inc_out, grad_out,
    own, field, grad, inc_sem, own_sem, out_sem,
):
    h = STEPS
    ext = cx + 2 * h
    ny = own.shape[2]
    nc = chan // CHUNKS
    tiles, _, cap, _ = back.shape
    slots = tiles * cap
    own_copy = pltpu.make_async_copy(control, own, own_sem)
    own_copy.start()
    inc_copy = pltpu.make_async_copy(inc_in, inc_out, inc_sem)
    inc_copy.start()
    eye = lax.broadcasted_iota(I32, (slots, slots), 0) == lax.broadcasted_iota(I32, (slots, slots), 1)
    for j, start, first, count in ((1, h, 0, cx), (0, h + cx, 0, h), (2, 0, cx - h, h)):
        rows_t = back[:, j].reshape(slots, chan).T
        lhs = jnp.concatenate(split(rows_t), axis=1)
        cell = jnp.sum(jnp.where(eye, cells[j, 0:1], 0), axis=1, keepdims=True)
        for x in range(0, count, 2):
            index = lax.broadcasted_iota(I32, (slots, 2 * ny), 1) + (first + x) * ny
            hot = jnp.where(index == cell, 1.0, 0.0).astype(BF16)
            out = jnp.dot(lhs, jnp.concatenate([hot, hot], axis=0), preferred_element_type=F32)
            field[start + x] = out[:, :ny]
            field[start + x + 1] = out[:, ny:]
    own_copy.wait()
    own2, grad2 = own.reshape(chan * cx, ny), grad.reshape(chan * cx, ny)
    copies = []
    for q in range(CHUNKS):

        @pl.loop(q * nc // 8, (q + 1) * nc // 8)
        def _(g):
            def load_row(i):
                return field[i, pl.ds(pl.multiple_of(g * 8, 8), 8), :]

            def emit(r, value):
                at = pl.ds(g * 8 * cx + r - h, 8, stride=cx)
                grad2[at, :] = own2[at, :] + ocb[r] * value

            sweep(load_row, fxb, fyb, emit, ext)

        part = pl.ds(q * nc, nc)
        copy = pltpu.make_async_copy(grad.at[part], grad_out.at[part], out_sem.at[q])
        copy.start()
        copies.append(copy)
    for copy in copies:
        copy.wait()
    inc_copy.wait()


def body(control, departures, obs_cell, obs_owner, scale_class, sea_mask, class_table, obs_precision):
    fields, levels, cx, ny = control.shape
    chan = fields * levels
    n = obs_cell.shape[0]
    tiles = lax.axis_size("tiles")
    cap = -(-max(2, 2 * n // tiles) // 8) * 8
    slots = tiles * cap
    ext = cx + 2 * STEPS
    flat = control.reshape(chan, cx, ny)
    vmem = pl.BlockSpec(memory_space=pltpu.VMEM)
    smem = pl.BlockSpec(memory_space=pltpu.SMEM)
    hbm = pl.BlockSpec(memory_space=pl.ANY)
    face = jax.ShapeDtypeStruct((ext, 8, ny), F32)
    state = jax.ShapeDtypeStruct((chan, cx, ny), F32)
    dma = pltpu.SemaphoreType.DMA
    inc, back, cells, fxb, fyb, ocb = pl.pallas_call(
        functools.partial(observe_kernel, tiles, cap, chan, cx),
        out_shape=(
            state,
            jax.ShapeDtypeStruct((tiles, 3, cap, chan), F32),
            jax.ShapeDtypeStruct((3, 8, slots), I32),
            face, face, face,
        ),
        in_specs=[smem, hbm] + [vmem] * 6,
        out_specs=(hbm, hbm, vmem, vmem, vmem, vmem),
        scratch_shapes=[
            pltpu.VMEM((chan, cx, ny), F32),
            pltpu.VMEM((chan, STEPS, ny), F32),
            pltpu.VMEM((chan, STEPS, ny), F32),
            pltpu.VMEM((chan, cx, ny), F32),
            pltpu.VMEM((2, cx, ny), I32),
            pltpu.VMEM((2, STEPS, ny), I32),
            pltpu.VMEM((2, STEPS, ny), I32),
            pltpu.VMEM((3, 8, slots), I32),
            pltpu.VMEM((2, 8, slots), I32),
            pltpu.VMEM((cx // 2, 2 * ny, slots), BF16),
            pltpu.VMEM((chan, slots), F32),
            pltpu.VMEM((tiles, cap, MEMBERS * chan), F32),
            pltpu.VMEM((tiles, cap, MEMBERS * chan), F32),
            pltpu.VMEM((tiles, cap, chan), F32),
            pltpu.VMEM((tiles, cap, chan), F32),
            pltpu.VMEM((tiles + 2, cap, chan), F32),
            pltpu.VMEM((tiles, 3, cap, chan), F32),
            pltpu.VMEM((MEMBERS, slots, chan), F32),
            dma, dma((CHUNKS,)), dma, dma((2, CHUNKS)), dma((2, CHUNKS)), dma((4,)), dma((4,)), dma((3,)), dma((3,)),
        ],
        compiler_params=pltpu.CompilerParams(
            collective_id=0, has_side_effects=True, vmem_limit_bytes=48 * 2**20
        ),
        name="observe",
    )(class_table, flat, departures, obs_cell.reshape(1, n), obs_owner.reshape(1, n), scale_class, sea_mask, obs_precision)
    increment, gradient = pl.pallas_call(
        functools.partial(adjoint_kernel, chan, cx),
        out_shape=(state, state),
        in_specs=[hbm, hbm] + [vmem] * 5,
        out_specs=(hbm, hbm),
        scratch_shapes=[
            pltpu.VMEM((chan, cx, ny), F32),
            pltpu.VMEM((ext, chan, ny), F32),
            pltpu.VMEM((chan, cx, ny), F32),
            dma, dma, dma((CHUNKS,)),
        ],
        compiler_params=pltpu.CompilerParams(vmem_limit_bytes=48 * 2**20),
        name="adjoint",
    )(flat, inc, back, cells, fxb, fyb, ocb)
    return increment.reshape(control.shape), gradient.reshape(control.shape)


def solution(mesh):
    return jax.shard_map(
        body,
        mesh=mesh,
        in_specs=(
            P("groups", None, "tiles", None),
            P(("groups", "tiles"), None),
            P(("groups", "tiles")),
            P(("groups", "tiles"), None),
            P("tiles", None),
            P("tiles", None),
            P(),
            P("tiles", None),
        ),
        out_specs=(P("groups", None, "tiles", None), P("groups", None, "tiles", None)),
        check_vma=False,
    )
```

profile of v0, /device:TPU:0, one launch (start us, length us, event | category | flops | bytes accessed | tf_op | source)
XLA Modules:
  0.0 105.1 jit_solution(4228631479560367835)
XLA Ops:
  0.6 0.0 copy-start
  0.6 1.4 %copy-done = f32[3,64,16,128]{3,2,1,0:T(8,128)S(1)} copy-done((f32[3,64,16,128]{3,2,1,0:T(8,128)S(1)}, f32[3,64,16,128]{3,2,1,0:T(8,128)}, u32[]{:S(2)}) %copy-start) | copy-done | bytes 1572888
  2.0 0.0 copy-start.2
  2.0 0.9 copy-done.2
  3.0 0.0 copy-start.3
  3.0 0.9 copy-done.3
  3.9 0.0 copy-start.4
  3.9 0.7 copy-done.4
  4.6 0.0 copy-start.5
  4.6 0.7 copy-done.5
  5.3 0.0 copy-start.6
  5.3 0.7 copy-done.6
  6.0 0.0 copy-start.7
  6.0 0.7 copy-done.7
  6.6 0.0 copy-start.8
  6.6 0.7 copy-done.8
  7.3 0.0 copy-start.1
  7.3 67.8 %observe.1 = (f32[192,16,128]{2,1,0:T(8,128)S(1)}, f32[16,3,8,192]{3,2,1,0:T(8,128)S(1)}, s32[3,8,128]{2,1,0:T(8,128)S(1)}, f32[32,8,128]{2,1,0:T(8,128)S(1)}, f...) custom-call(f32[2,8]{1,0:T(2,128)S(1)} %copy-done.6, f32[192,16,128]{2,1,0:T(8,128)S(1)} %bitcast.5, ...), custom_call_target="tpu_custom_call" | custom-call | tf_op jit(solution)/shard_map/observe/pallas_call | solution.py:308
  75.1 0.0 copy-done.1
  75.1 29.9 %adjoint.1 = (f32[192,16,128]{2,1,0:T(8,128)}, f32[192,16,128]{2,1,0:T(8,128)}) custom-call(f32[192,16,128]{2,1,0:T(8,128)S(1)} %bitcast.6, f32[192,16,128]{2,1,0:T(8,128)S(1)} %get-tuple-element.10.inc_in, f32[16,3,8,192]{3,2,1,0:T(8,128)S(1)} %get-tuple-element.11.back, s32[3,8,128]{2,1,0:T(8,128)S(1)} %get-tuple-element.12.cells, ...), custom_call_target="tpu_custom_call" | custom-call | tf_op jit(solution)/shard_map/adjoint/pallas_call | solution.py:344
Async XLA Ops:
  0.6 1.4 %copy-start = (f32[3,64,16,128]{3,2,1,0:T(8,128)S(1)}, f32[3,64,16,128]{3,2,1,0:T(8,128)}, u32[]{:S(2)}) copy-start(f32[3,64,16,128]{3,2,1,0:T(8,128)} %param.8) | copy-start | bytes 4718596
  2.0 0.9 copy-start.2
  3.0 0.9 copy-start.3
  3.9 0.7 copy-start.4
  4.6 0.7 copy-start.5
  5.3 0.7 copy-start.6
  6.0 0.7 copy-start.7
  6.6 0.7 copy-start.8
  7.3 67.9 %copy-start.1 = (f32[3,64,16,128]{3,2,1,0:T(8,128)S(1)}, f32[3,64,16,128]{3,2,1,0:T(8,128)}, u32[]{:S(2)}) copy-start(f32[3,64,16,128]{3,2,1,0:T(8,128)} %param.8) | copy-start | bytes 4718596
where the time goes:
time: 105 us
  Pallas kernels  97.8 us (93%)
  local copies, waits for them, and re-layouts  6.64 us (6%)
    pallas_call x1, Pallas kernels, body(): pl.pallas_call(functools.partial(observe_kernel, tiles, cap, chan, cx), o...  67.8 us
    pallas_call x1, Pallas kernels, body(): pl.pallas_call(functools.partial(adjoint_kernel, chan, cx), out_shape=(st...  29.9 us
    unnamed x18, local copies, waits for them, and re-layouts  6.64 us

commit v1 on v0

--- a/solution.py
+++ b/solution.py
@@ -15,35 +15,45 @@
 I32 = jnp.int32
 
 
-def sweep(load_row, fx_ref, fy_ref, emit, rows):
-    current = [None] * (STEPS + 1)
-    flux = [None] * (STEPS + 1)
-    for i in range(rows):
-        value = load_row(i)
-        for s in range(1, STEPS + 1):
-            before, current[s] = current[s], value
-            if before is None:
-                break
-            r = i - s
-            flux_x = fx_ref[r] * (value - before)
-            last, flux[s] = flux[s], flux_x
-            if last is None:
-                break
-            flux_y = fy_ref[r] * (pltpu.roll(before, before.shape[1] - 1, 1) - before)
-            value = before + ((flux_x - last) + (flux_y - pltpu.roll(flux_y, 1, 1)))
-        else:
-            emit(i - STEPS, value)
-
-
 def split(x):
     high = x.astype(BF16)
     return high, (x - high.astype(F32)).astype(BF16)
 
 
+def shifts(ny):
+    row = lax.broadcasted_iota(I32, (ny, ny), 0)
+    col = lax.broadcasted_iota(I32, (ny, ny), 1)
+    both = jnp.concatenate(
+        [jnp.where(row == col + 1, 1.0, 0.0).astype(BF16), jnp.where(row + 1 == col, 1.0, 0.0).astype(BF16)], axis=1
+    )
+    return jnp.concatenate([both, both], axis=0)
+
+
+def sweep(state, faces, shift):
+    count, ny = state[0].shape
+
+    def face(which, r):
+        return jnp.concatenate([faces[which, r]] * (count // 8), axis=0)
+
+    for s in range(1, STEPS + 1):
+        m = len(state)
+        flux = [face(0, s - 1 + i) * (state[i + 1] - state[i]) for i in range(m - 1)]
+        inner = jnp.concatenate(state[1:-1], axis=0)
+        beside = jnp.dot(jnp.concatenate(split(inner), axis=1), shift, preferred_element_type=F32)
+        after = []
+        for i in range(1, m - 1):
+            here = state[i]
+            pair = beside[(i - 1) * count : i * count]
+            change_y = face(1, s - 1 + i) * (pair[:, :ny] - here) + face(2, s - 1 + i) * (pair[:, ny:] - here)
+            after.append(here + ((flux[i] - flux[i - 1]) + change_y))
+        state = after
+    return state
+
+
 def observe_kernel(
     tiles, cap, chan, cx,
     table, control, departures, cell_ref, owner_ref, class_ref, mask_ref, precision_ref,
-    inc_out, back_out, cells_out, fxb, fyb, ocb,
+    inc_out, back_out, cells_out, faces, ocb,
     own, halo_l, halo_r, inc, geo, geo_l, geo_r, cells, cells_in, hot, model_t,
     dep_send, dep_recv, mod_send, mod_recv, ans, back, weighted_dep,
     local_sem, out_sem, back_sem, halo_send, halo_recv, geo_send, geo_recv, a2a_send, a2a_recv,
@@ -82,16 +92,15 @@
     ]
     for copy in geo_copies:
         copy.start()
-    halo_copies = []
+    def halo_copy(side, q):
+        part = pl.ds(q * nc, nc)
+        if side == 0:
+            return remote(control.at[part, pl.ds(cx - h, h)], halo_l.at[part], halo_send.at[0, q], halo_recv.at[0, q], right)
+        return remote(control.at[part, pl.ds(0, h)], halo_r.at[part], halo_send.at[1, q], halo_recv.at[1, q], left)
+
     for q in range(CHUNKS):
-        part = pl.ds(q * nc, nc)
-        pair = [
-            remote(control.at[part, pl.ds(cx - h, h)], halo_l.at[part], halo_send.at[0, q], halo_recv.at[0, q], right),
-            remote(control.at[part, pl.ds(0, h)], halo_r.at[part], halo_send.at[1, q], halo_recv.at[1, q], left),
-        ]
-        for copy in pair:
-            copy.start()
-        halo_copies.append(pair)
+        for side in range(2):
+            halo_copy(side, q).start()
 
     n = departures.shape[0]
     eye = lax.broadcasted_iota(I32, (n, n), 0) == lax.broadcasted_iota(I32, (n, n), 1)
@@ -152,46 +161,40 @@
     face_x = 0.5 * (kx + pltpu.roll(kx, ext - 1, 0)) * ocean * pltpu.roll(ocean, ext - 1, 0)
     face_y = 0.5 * (ky + pltpu.roll(ky, ny - 1, 1)) * ocean * pltpu.roll(ocean, ny - 1, 1)
     face_y = jnp.where(lax.broadcasted_iota(I32, (ext, ny), 1) < ny - 1, face_y, 0.0)
+    face_w = pltpu.roll(face_y, 1, 1)
     for r in range(ext):
-        fxb[r] = jnp.broadcast_to(face_x[r : r + 1], (8, ny))
-        fyb[r] = jnp.broadcast_to(face_y[r : r + 1], (8, ny))
+        for which, array in enumerate((face_x, face_y, face_w)):
+            faces[which, r] = jnp.broadcast_to(array[r : r + 1], (8, ny))
         ocb[r] = jnp.broadcast_to(ocean[r : r + 1], (8, ny))
 
     own_copy.wait()
     own2, left2, right2, inc2 = (
         own.reshape(chan * cx, ny), halo_l.reshape(chan * h, ny), halo_r.reshape(chan * h, ny), inc.reshape(chan * cx, ny)
     )
-    inc_copies = []
-    for q in range(CHUNKS):
-        for copy in halo_copies[q]:
-            copy.wait_recv()
-
-        @pl.loop(q * nc // 8, (q + 1) * nc // 8)
-        def _(g):
-            def load_row(i):
-                if i < h:
-                    row = left2[pl.ds(g * 8 * h + i, 8, stride=h), :]
-                elif i < h + cx:
-                    row = own2[pl.ds(g * 8 * cx + i - h, 8, stride=cx), :]
-                else:
-                    row = right2[pl.ds(g * 8 * h + i - h - cx, 8, stride=h), :]
-                return ocb[i] * row
-
-            def emit(r, value):
-                inc2[pl.ds(g * 8 * cx + r - h, 8, stride=cx), :] = value
-
-            sweep(load_row, fxb, fyb, emit, ext)
-
+    shift = shifts(ny)
+
+    @pl.loop(0, CHUNKS)
+    def _(q):
+        halo_copy(0, q).wait_recv()
+        halo_copy(1, q).wait_recv()
+
+        def load_row(i):
+            if i < h:
+                row = left2[pl.ds(q * nc * h + i, nc, stride=h), :]
+            elif i < h + cx:
+                row = own2[pl.ds(q * nc * cx + i - h, nc, stride=cx), :]
+            else:
+                row = right2[pl.ds(q * nc * h + i - h - cx, nc, stride=h), :]
+            return jnp.concatenate([ocb[i]] * (nc // 8), axis=0) * row
+
+        rows = sweep([load_row(i) for i in range(ext)], faces, shift)
+        for r in range(cx):
+            inc2[pl.ds(q * nc * cx + r, nc, stride=cx), :] = rows[r]
         part = pl.ds(q * nc, nc)
-        copy = pltpu.make_async_copy(inc.at[part], inc_out.at[part], out_sem.at[q])
-        copy.start()
-        inc_copies.append(copy)
+        pltpu.make_async_copy(inc.at[part], inc_out.at[part], out_sem.at[q]).start()
         total = jnp.zeros((nc, slots), F32)
         for j in range(cx // 2):
-            pair = jnp.concatenate(
-                [inc2[pl.ds(q * nc * cx + 2 * j + b, nc, stride=cx), :] for b in range(2)], axis=1
-            )
-            for piece in split(pair):
+            for piece in split(jnp.concatenate(rows[2 * j : 2 * j + 2], axis=1)):
                 total += jnp.dot(piece, hot[j], preferred_element_type=F32)
         model_t[part] = total
 
@@ -224,13 +227,14 @@
     cells_out[0] = cells_in[0]
     cells_out[1] = cells[1]
     cells_out[2] = cells_in[1]
-    for pair in halo_copies:
-        for copy in pair:
-            copy.wait_send()
+    for q in range(CHUNKS):
+        for side in range(2):
+            halo_copy(side, q).wait_send()
     landed(dep_recv, a2a_send.at[0])
     landed(mod_recv, a2a_send.at[1])
-    for copy in inc_copies:
-        copy.wait()
+    for q in range(CHUNKS):
+        part = pl.ds(q * nc, nc)
+        pltpu.make_async_copy(inc.at[part], inc_out.at[part], out_sem.at[q]).wait()
     landed(back, a2a_recv.at[2])
     landed(back, a2a_send.at[2])
     copy = pltpu.make_async_copy(back, back_out, back_sem)
@@ -240,7 +244,7 @@
 
 def adjoint_kernel(
     chan, cx,
-    control, inc_in, back, cells, fxb, fyb, ocb,
+    control, inc_in, back, cells, faces, ocb,
     inc_out, grad_out,
     own, field, grad, inc_sem, own_sem, out_sem,
 ):
@@ -267,26 +271,22 @@
             field[start + x + 1] = out[:, ny:]
     own_copy.wait()
     own2, grad2 = own.reshape(chan * cx, ny), grad.reshape(chan * cx, ny)
-    copies = []
+    shift = shifts(ny)
+
+    def out_copy(q):
+        part = pl.ds(q * nc, nc)
+        return pltpu.make_async_copy(grad.at[part], grad_out.at[part], out_sem.at[q])
+
+    @pl.loop(0, CHUNKS)
+    def _(q):
+        rows = sweep([field[i, pl.ds(pl.multiple_of(q * nc, nc), nc), :] for i in range(ext)], faces, shift)
+        for r in range(cx):
+            at = pl.ds(q * nc * cx + r, nc, stride=cx)
+            grad2[at, :] = own2[at, :] + jnp.concatenate([ocb[r + h]] * (nc // 8), axis=0) * rows[r]
+        out_copy(q).start()
+
     for q in range(CHUNKS):
-
-        @pl.loop(q * nc // 8, (q + 1) * nc // 8)
-        def _(g):
-            def load_row(i):
-                return field[i, pl.ds(pl.multiple_of(g * 8, 8), 8), :]
-
-            def emit(r, value):
-                at = pl.ds(g * 8 * cx + r - h, 8, stride=cx)
-                grad2[at, :] = own2[at, :] + ocb[r] * value
-
-            sweep(load_row, fxb, fyb, emit, ext)
-
-        part = pl.ds(q * nc, nc)
-        copy = pltpu.make_async_copy(grad.at[part], grad_out.at[part], out_sem.at[q])
-        copy.start()
-        copies.append(copy)
-    for copy in copies:
-        copy.wait()
+        out_copy(q).wait()
     inc_copy.wait()
 
 
@@ -302,19 +302,19 @@
     vmem = pl.BlockSpec(memory_space=pltpu.VMEM)
     smem = pl.BlockSpec(memory_space=pltpu.SMEM)
     hbm = pl.BlockSpec(memory_space=pl.ANY)
-    face = jax.ShapeDtypeStruct((ext, 8, ny), F32)
     state = jax.ShapeDtypeStruct((chan, cx, ny), F32)
     dma = pltpu.SemaphoreType.DMA
-    inc, back, cells, fxb, fyb, ocb = pl.pallas_call(
+    inc, back, cells, faces, ocb = pl.pallas_call(
         functools.partial(observe_kernel, tiles, cap, chan, cx),
         out_shape=(
             state,
             jax.ShapeDtypeStruct((tiles, 3, cap, chan), F32),
             jax.ShapeDtypeStruct((3, 8, slots), I32),
-            face, face, face,
+            jax.ShapeDtypeStruct((3, ext, 8, ny), F32),
+            jax.ShapeDtypeStruct((ext, 8, ny), F32),
         ),
         in_specs=[smem, hbm] + [vmem] * 6,
-        out_specs=(hbm, hbm, vmem, vmem, vmem, vmem),
+        out_specs=(hbm, hbm, vmem, vmem, vmem),
         scratch_shapes=[
             pltpu.VMEM((chan, cx, ny), F32),
             pltpu.VMEM((chan, STEPS, ny), F32),
@@ -337,14 +337,14 @@
             dma, dma((CHUNKS,)), dma, dma((2, CHUNKS)), dma((2, CHUNKS)), dma((4,)), dma((4,)), dma((3,)), dma((3,)),
         ],
         compiler_params=pltpu.CompilerParams(
-            collective_id=0, has_side_effects=True, vmem_limit_bytes=48 * 2**20
+            collective_id=0, has_side_effects=True, vmem_limit_bytes=63 * 2**20
         ),
         name="observe",
     )(class_table, flat, departures, obs_cell.reshape(1, n), obs_owner.reshape(1, n), scale_class, sea_mask, obs_precision)
     increment, gradient = pl.pallas_call(
         functools.partial(adjoint_kernel, chan, cx),
         out_shape=(state, state),
-        in_specs=[hbm, hbm] + [vmem] * 5,
+        in_specs=[hbm, hbm] + [vmem] * 4,
         out_specs=(hbm, hbm),
         scratch_shapes=[
             pltpu.VMEM((chan, cx, ny), F32),
@@ -352,9 +352,9 @@
             pltpu.VMEM((chan, cx, ny), F32),
             dma, dma, dma((CHUNKS,)),
         ],
-        compiler_params=pltpu.CompilerParams(vmem_limit_bytes=48 * 2**20),
+        compiler_params=pltpu.CompilerParams(vmem_limit_bytes=63 * 2**20),
         name="adjoint",
-    )(flat, inc, back, cells, fxb, fyb, ocb)
+    )(flat, inc, back, cells, faces, ocb)
     return increment.reshape(control.shape), gradient.reshape(control.shape)
 
 

time: 105 us -> 101 us (0.962)
  local copies, waits for them, and re-layouts: 6.64 us -> 0 us
  Pallas kernels: 97.8 us -> 100 us
    pallas_call x1, Pallas kernels: 29.9 us -> 50 us  [body(): pl.pallas_call(functools.partial(adjoint_kernel, chan, cx), out_shape=(st...]
    pallas_call x1, Pallas kernels: 67.8 us -> 50.4 us  [body(): pl.pallas_call(functools.partial(observe_kernel, tiles, cap, chan, cx), o...]
    unnamed x18 -> x0, local copies, waits for them, and re-layouts: 6.64 us -> none
where the time goes in v1:
time: 101 us
  Pallas kernels  100 us (99%)
    pallas_call x1, Pallas kernels, body(): pl.pallas_call(functools.partial(observe_kernel, tiles, cap, chan, cx), o...  50.4 us
    pallas_call x1, Pallas kernels, body(): pl.pallas_call(functools.partial(adjoint_kernel, chan, cx), out_shape=(st...  50 us

profile of v1, /device:TPU:0, one launch (start us, length us, event | category | flops | bytes accessed | tf_op | source)
XLA Modules:
  0.0 101.0 jit_solution(11109679756728355990)
XLA Ops:
  0.6 50.4 %observe.1 = (f32[192,16,128]{2,1,0:T(8,128)}, f32[16,3,8,192]{3,2,1,0:T(8,128)}, s32[3,8,128]{2,1,0:T(8,128)}, f32[3,32,8,128]{3,2,1,0:T(8,128)}, f32[32,8,128]{2,1,0:T(8,128)}) custom-call(f32[2,8]{1,0:T(2,128)} %table.1, f32[192,16,128]{2,1,0:T(8,128)} %bitcast.5, f32[64,768]{1,0:T(8,128)} %departures.1, s32[1,64]{1,0:T(1,128)} %bitcast.7, ...), custom_call_target="tpu_custom_call" | custom-call | tf_op jit(solution)/shard_map/observe/pallas_call | solution.py:307
  51.1 50.0 %adjoint.1 = (f32[192,16,128]{2,1,0:T(8,128)}, f32[192,16,128]{2,1,0:T(8,128)}) custom-call(f32[192,16,128]{2,1,0:T(8,128)} %bitcast.6, f32[192,16,128]{2,1,0:T(8,128)} %get-tuple-element.9.inc_in, f32[16,3,8,192]{3,2,1,0:T(8,128)} %get-tuple-element.10.back, s32[3,8,128]{2,1,0:T(8,128)} %get-tuple-element.11.cells, ...), custom_call_target="tpu_custom_call" | custom-call | tf_op jit(solution)/shard_map/adjoint/pallas_call | solution.py:344

commit v2 on v1

--- a/solution.py
+++ b/solution.py
@@ -246,7 +246,7 @@
     chan, cx,
     control, inc_in, back, cells, faces, ocb,
     inc_out, grad_out,
-    own, field, grad, inc_sem, own_sem, out_sem,
+    own, field, grad, inc, inc_sem, own_sem, out_sem,
 ):
     h = STEPS
     ext = cx + 2 * h
@@ -256,7 +256,7 @@
     slots = tiles * cap
     own_copy = pltpu.make_async_copy(control, own, own_sem)
     own_copy.start()
-    inc_copy = pltpu.make_async_copy(inc_in, inc_out, inc_sem)
+    inc_copy = pltpu.make_async_copy(inc_in, inc, inc_sem)
     inc_copy.start()
     eye = lax.broadcasted_iota(I32, (slots, slots), 0) == lax.broadcasted_iota(I32, (slots, slots), 1)
     for j, start, first, count in ((1, h, 0, cx), (0, h + cx, 0, h), (2, 0, cx - h, h)):
@@ -270,6 +270,9 @@
             field[start + x] = out[:, :ny]
             field[start + x + 1] = out[:, ny:]
     own_copy.wait()
+    inc_copy.wait()
+    inc_copy = pltpu.make_async_copy(inc, inc_out, inc_sem)
+    inc_copy.start()
     own2, grad2 = own.reshape(chan * cx, ny), grad.reshape(chan * cx, ny)
     shift = shifts(ny)
 
@@ -350,6 +353,7 @@
             pltpu.VMEM((chan, cx, ny), F32),
             pltpu.VMEM((ext, chan, ny), F32),
             pltpu.VMEM((chan, cx, ny), F32),
+            pltpu.VMEM((chan, cx, ny), F32),
             dma, dma, dma((CHUNKS,)),
         ],
         compiler_params=pltpu.CompilerParams(vmem_limit_bytes=63 * 2**20),

time: 101 us -> 64.6 us (0.64)
  Pallas kernels: 100 us -> 63.8 us
    pallas_call x1, Pallas kernels: 50 us -> 13.3 us  [body(): pl.pallas_call(functools.partial(adjoint_kernel, chan, cx), out_shape=(st...]
where the time goes in v2:
time: 64.6 us; the launch traced here: 64.4 us
  Pallas kernels  63.8 us (99%)
    pallas_call x1, Pallas kernels, body(): pl.pallas_call(functools.partial(observe_kernel, tiles, cap, chan, cx), o...  50.4 us
    pallas_call x1, Pallas kernels, body(): pl.pallas_call(functools.partial(adjoint_kernel, chan, cx), out_shape=(st...  13.3 us

profile of v2, /device:TPU:0, one launch (start us, length us, event | category | flops | bytes accessed | tf_op | source)
XLA Modules:
  0.0 64.4 jit_solution(15499375689653200069)
XLA Ops:
  0.6 50.4 %observe.1 = (f32[192,16,128]{2,1,0:T(8,128)}, f32[16,3,8,192]{3,2,1,0:T(8,128)}, s32[3,8,128]{2,1,0:T(8,128)}, f32[3,32,8,128]{3,2,1,0:T(8,128)}, f32[32,8,128]{2,1,0:T(8,128)}) custom-call(f32[2,8]{1,0:T(2,128)} %table.1, f32[192,16,128]{2,1,0:T(8,128)} %bitcast.5, f32[64,768]{1,0:T(8,128)} %departures.1, s32[1,64]{1,0:T(1,128)} %bitcast.7, ...), custom_call_target="tpu_custom_call" | custom-call | tf_op jit(solution)/shard_map/observe/pallas_call | solution.py:310
  51.1 13.3 %adjoint.1 = (f32[192,16,128]{2,1,0:T(8,128)}, f32[192,16,128]{2,1,0:T(8,128)}) custom-call(f32[192,16,128]{2,1,0:T(8,128)} %bitcast.6, f32[192,16,128]{2,1,0:T(8,128)} %get-tuple-element.9.inc_in, f32[16,3,8,192]{3,2,1,0:T(8,128)} %get-tuple-element.10.back, s32[3,8,128]{2,1,0:T(8,128)} %get-tuple-element.11.cells, ...), custom_call_target="tpu_custom_call" | custom-call | tf_op jit(solution)/shard_map/adjoint/pallas_call | solution.py:347

commit v3 on v2

--- a/solution.py
+++ b/solution.py
@@ -55,7 +55,7 @@
     table, control, departures, cell_ref, owner_ref, class_ref, mask_ref, precision_ref,
     inc_out, back_out, cells_out, faces, ocb,
     own, halo_l, halo_r, inc, geo, geo_l, geo_r, cells, cells_in, hot, model_t,
-    dep_send, dep_recv, mod_send, mod_recv, ans, back, weighted_dep,
+    dep_send, dep_recv, mod_send, mod_recv, ans, back, back_l, back_r, weighted_dep,
     local_sem, out_sem, back_sem, halo_send, halo_recv, geo_send, geo_recv, a2a_send, a2a_recv,
 ):
     me = lax.axis_index("tiles")
@@ -134,11 +134,9 @@
     def cell_row(dest):
         return jnp.sum(jnp.where(dest == slot_lane, cell_col + 1, 0), axis=0, keepdims=True) - 1
 
-    later = jnp.where(offset + 1 == tiles, 0, offset + 1) * cap + slot_col
-    sooner = jnp.where(offset == 0, tiles - 1, offset - 1) * cap + slot_col
     mine = cell_row(dest_col)
-    for j, row in enumerate((cell_row(later), mine, cell_row(sooner))):
-        cells[j] = jnp.broadcast_to(row, cells.shape[1:])
+    for j in range(3):
+        cells[j] = jnp.broadcast_to(mine, cells.shape[1:])
     cell_copies = [
         remote(cells.at[0], cells_in.at[0], geo_send.at[2], geo_recv.at[2], left),
         remote(cells.at[2], cells_in.at[1], geo_send.at[3], geo_recv.at[3], right),
@@ -215,13 +213,9 @@
         weighted = weighted_model - weighted_dep[m]
         energy = jnp.sum(misfit * weighted, axis=1, keepdims=True) / chan
         answer += weighted / (1.0 + energy)
-    answer = answer.reshape(tiles, cap, chan)
-    ans[pl.ds(1, tiles)] = answer
-    ans[0] = answer[tiles - 1]
-    ans[tiles + 1] = answer[0]
-    exchange(lambda k: (ans.at[pl.ds(k, 3)], lax.rem(me - k + tiles, tiles)), back, 2)
-    for j in range(3):
-        back[0, j] = ans[j]
+    ans[...] = answer.reshape(tiles, cap, chan)
+    exchange(lambda k: (ans.at[k], lax.rem(me - k + tiles, tiles)), back, 2)
+    back[0] = ans[0]
     for copy in cell_copies:
         copy.wait()
     cells_out[0] = cells_in[0]
@@ -236,10 +230,22 @@
         part = pl.ds(q * nc, nc)
         pltpu.make_async_copy(inc.at[part], inc_out.at[part], out_sem.at[q]).wait()
     landed(back, a2a_recv.at[2])
+    forward = [
+        remote(back, back_r, geo_send.at[4], geo_recv.at[4], left),
+        remote(back, back_l, geo_send.at[5], geo_recv.at[5], right),
+    ]
+    for copy in forward:
+        copy.start()
     landed(back, a2a_send.at[2])
-    copy = pltpu.make_async_copy(back, back_out, back_sem)
-    copy.start()
-    copy.wait()
+    out = [pltpu.make_async_copy(back, back_out.at[1], back_sem.at[1])]
+    out[0].start()
+    for copy in forward:
+        copy.wait()
+    for j, buffer in ((0, back_r), (2, back_l)):
+        out.append(pltpu.make_async_copy(buffer, back_out.at[j], back_sem.at[j]))
+        out[-1].start()
+    for copy in out:
+        copy.wait()
 
 
 def adjoint_kernel(
@@ -252,7 +258,7 @@
     ext = cx + 2 * h
     ny = own.shape[2]
     nc = chan // CHUNKS
-    tiles, _, cap, _ = back.shape
+    _, tiles, cap, _ = back.shape
     slots = tiles * cap
     own_copy = pltpu.make_async_copy(control, own, own_sem)
     own_copy.start()
@@ -260,7 +266,7 @@
     inc_copy.start()
     eye = lax.broadcasted_iota(I32, (slots, slots), 0) == lax.broadcasted_iota(I32, (slots, slots), 1)
     for j, start, first, count in ((1, h, 0, cx), (0, h + cx, 0, h), (2, 0, cx - h, h)):
-        rows_t = back[:, j].reshape(slots, chan).T
+        rows_t = back[j].reshape(slots, chan).T
         lhs = jnp.concatenate(split(rows_t), axis=1)
         cell = jnp.sum(jnp.where(eye, cells[j, 0:1], 0), axis=1, keepdims=True)
         for x in range(0, count, 2):
@@ -311,7 +317,7 @@
         functools.partial(observe_kernel, tiles, cap, chan, cx),
         out_shape=(
             state,
-            jax.ShapeDtypeStruct((tiles, 3, cap, chan), F32),
+            jax.ShapeDtypeStruct((3, tiles, cap, chan), F32),
             jax.ShapeDtypeStruct((3, 8, slots), I32),
             jax.ShapeDtypeStruct((3, ext, 8, ny), F32),
             jax.ShapeDtypeStruct((ext, 8, ny), F32),
@@ -334,10 +340,12 @@
             pltpu.VMEM((tiles, cap, MEMBERS * chan), F32),
             pltpu.VMEM((tiles, cap, chan), F32),
             pltpu.VMEM((tiles, cap, chan), F32),
-            pltpu.VMEM((tiles + 2, cap, chan), F32),
-            pltpu.VMEM((tiles, 3, cap, chan), F32),
+            pltpu.VMEM((tiles, cap, chan), F32),
+            pltpu.VMEM((tiles, cap, chan), F32),
+            pltpu.VMEM((tiles, cap, chan), F32),
+            pltpu.VMEM((tiles, cap, chan), F32),
             pltpu.VMEM((MEMBERS, slots, chan), F32),
-            dma, dma((CHUNKS,)), dma, dma((2, CHUNKS)), dma((2, CHUNKS)), dma((4,)), dma((4,)), dma((3,)), dma((3,)),
+            dma, dma((CHUNKS,)), dma((3,)), dma((2, CHUNKS)), dma((2, CHUNKS)), dma((6,)), dma((6,)), dma((3,)), dma((3,)),
         ],
         compiler_params=pltpu.CompilerParams(
             collective_id=0, has_side_effects=True, vmem_limit_bytes=63 * 2**20

time: 64.6 us -> 62.9 us (0.974); the launches traced: 64.4 us -> 61.9 us
  Pallas kernels: 63.8 us -> 61.2 us
    pallas_call x1, Pallas kernels: 50.4 us -> 47.9 us  [body(): pl.pallas_call(functools.partial(observe_kernel, tiles, cap, chan, cx), o...]
where the time goes in v3:
time: 62.9 us; the launch traced here: 61.9 us
  Pallas kernels  61.2 us (97%)
  between operations  0.64 us (1%)
    pallas_call x1, Pallas kernels, body(): pl.pallas_call(functools.partial(observe_kernel, tiles, cap, chan, cx), o...  47.9 us
    pallas_call x1, Pallas kernels, body(): pl.pallas_call(functools.partial(adjoint_kernel, chan, cx), out_shape=(st...  13.3 us

profile of v3, /device:TPU:0, one launch (start us, length us, event | category | flops | bytes accessed | tf_op | source)
XLA Modules:
  0.0 61.9 jit_solution(6140278835136365171)
XLA Ops:
  0.6 47.9 %observe.1 = (f32[192,16,128]{2,1,0:T(8,128)}, f32[3,16,8,192]{3,2,1,0:T(8,128)}, s32[3,8,128]{2,1,0:T(8,128)}, f32[3,32,8,128]{3,2,1,0:T(8,128)}, f32[32,8,128]{2,1,0:T(8,128)}) custom-call(f32[2,8]{1,0:T(2,128)} %table.1, f32[192,16,128]{2,1,0:T(8,128)} %bitcast.5, f32[64,768]{1,0:T(8,128)} %departures.1, s32[1,64]{1,0:T(1,128)} %bitcast.7, ...), custom_call_target="tpu_custom_call" | custom-call | tf_op jit(solution)/shard_map/observe/pallas_call | solution.py:316
  48.5 13.3 %adjoint.1 = (f32[192,16,128]{2,1,0:T(8,128)}, f32[192,16,128]{2,1,0:T(8,128)}) custom-call(f32[192,16,128]{2,1,0:T(8,128)} %bitcast.6, f32[192,16,128]{2,1,0:T(8,128)} %get-tuple-element.9.inc_in, f32[3,16,8,192]{3,2,1,0:T(8,128)} %get-tuple-element.10.back, s32[3,8,128]{2,1,0:T(8,128)} %get-tuple-element.11.cells, ...), custom_call_target="tpu_custom_call" | custom-call | tf_op jit(solution)/shard_map/adjoint/pallas_call | solution.py:355
